TPU v7x, 32 devices: a whole 2x2x4 slice. The times are simulated.
32 devices in a mesh: grp: 2 (over y), lon: 8 (over z, x), lat: 2 (over core).
Axes of the slice: x: 2, y: 2, z: 4, core: 2. Of those that a mesh axis runs over, the one named last changes fastest.
Arguments:
- state: float32 [5, 192, 64], P(None, ('grp', 'lon'), 'lat'), parts along dimension 1, may hold values from -4 to 4
- target: float32 [5, 192, 64], P(None, ('grp', 'lon'), 'lat'), parts along dimension 1, may hold values from -4 to 4
- depth: float32 [192, 64], P(('grp', 'lon'), 'lat'), parts along dimension 0, may hold values from 0.5 to 1.5
- land_mask: int32 [192, 64], P(('grp', 'lon'), 'lat'), parts along dimension 0, may hold values from 0 to 1, as said below
- w_one: float32 [45, 256], replicated, may hold values from -0.875 to 0.875
- b_one: float32 [256], replicated, may hold values from -3 to 3
- w_two: float32 [256, 256], replicated, may hold values from -0.375 to 0.375
- b_two: float32 [256], replicated, may hold values from -3 to 3
- w_three: float32 [256, 5], replicated, may hold values from -0.375 to 0.375
- b_three: float32 [5], replicated, may hold values from -3 to 3
Outputs:
- loss_value: float32 [2], P('grp'), parts along dimension 0
- state_adjoint: float32 [5, 192, 64], P(None, ('grp', 'lon'), 'lat'), parts along dimension 1
- direction_w_one: float32 [90, 256], P('grp'), parts along dimension 0
- direction_b_one: float32 [512], P('grp'), parts along dimension 0
- direction_w_two: float32 [512, 256], P('grp'), parts along dimension 0
- direction_b_two: float32 [512], P('grp'), parts along dimension 0
- direction_w_three: float32 [512, 5], P('grp'), parts along dimension 0
- direction_b_three: float32 [10], P('grp'), parts along dimension 0
There are 2 independent parts, one for each index of `grp`. A program takes and returns all parts, laid end to end along the dimension named above; an argument that names none is the same for every part. Nothing has to cross between parts.
Inputs may be any that keep to these rules, and one draw needn't show every extreme that they name: `land_mask`: land is drawn cell by cell; in alternate eighths of the longitudes about 70 and about 15 percent of the cells are land.
All inputs are finite; a program needn't handle non-finite values.
Results may differ from a plain program's by a relative error of at most 0.0001.
Values sent between devices are 32-bit elements; how exact they have to be, the bound alone decides.
A program may use at most 64 MiB of HBM per device.

v0:
```python
import functools

import jax
import jax.numpy as jnp
from jax import lax
from jax.experimental import pallas as pl
from jax.experimental.pallas import tpu as pltpu
from jax.sharding import PartitionSpec as P

STEPS = 2
LEVELS = 3 * STEPS
HID = 256
FROWS = 80
time_step = 0.4
eps_norm = 1e-06
f32 = jnp.float32
bf16 = jnp.bfloat16
MESH = pl.DeviceIdType.MESH


def split(value):
    high = value.astype(bf16)
    low = (value - high.astype(f32)).astype(bf16)
    return high, low


def matmul(left, right):
    return jnp.dot(left, right, preferred_element_type=f32)


def matmul_t(left, right):
    return lax.dot_general(left, right, (((1,), (1,)), ((), ())), preferred_element_type=f32)


def stacked(value):
    high, low = split(value)
    return jnp.concatenate([high, low, high], axis=0)


def kernel(
    peers, chunk, row, number, cells_total,
    field_ref, w1_ref, w2_ref, w3t_ref, b2_ref, b3_ref,
    loss_out, adj_out, w1_out, b1_out, w2_out, b2_out, w3_out, b3_out,
    part_buf, edge_send, edge_recv, tape_f, tape_h1, tape_h2,
    w1_fwd, w1_bwd, w2_fwd, w2_bwd, w3_fwd, w3_bwd,
    acc_w1, acc_w2, acc_w3, acc_b2, acc_b3,
    grad_buf, reduce_buf, gather_buf,
    part_sem, edge_ssem, edge_rsem, back_sem, rs_ssem, rs_rsem, ag_ssem, ag_rsem,
):
    grp = lax.axis_index("grp")
    lon = lax.axis_index("lon")
    half = lax.axis_index("lat")
    me = lon * 2 + half

    def place(position):
        return (grp, position // 2, position % 2)

    east = place((me + 1) % peers)
    west = place((me + peers - 1) % peers)
    partner = (grp, lon, 1 - half)

    barrier = pltpu.get_barrier_semaphore()

    def greet(step, carry):
        pl.semaphore_signal(barrier, inc=1, device_id=place((me + step) % peers), device_id_type=MESH)
        return carry

    lax.fori_loop(1, peers, greet, 0, unroll=peers <= 16)
    pl.semaphore_wait(barrier, peers - 1)

    first = pltpu.make_async_remote_copy(
        src_ref=field_ref.at[1 - half], dst_ref=part_buf,
        send_sem=part_sem.at[0], recv_sem=part_sem.at[1],
        device_id=partner, device_id_type=MESH,
    )
    first.start()

    lanes = field_ref.shape[2]
    lane = lax.broadcasted_iota(jnp.int32, (8, lanes), 1)
    sub = lax.broadcasted_iota(jnp.int32, (8, lanes), 0)
    latitude = lane % row
    low_edge = latitude == 0
    high_edge = latitude == row - 1
    lane_tile = lax.broadcasted_iota(jnp.int32, (8, 128), 1)
    lower_half = lane_tile < row
    coriolis = (0.2 + 0.6 * (latitude.astype(f32) + 0.5) / row)[0:1]

    w1 = w1_ref[...]
    high, low = split(w1)
    w1_bwd[...] = jnp.concatenate([high, high, low], axis=1)
    high, low = high.astype(f32), low.astype(f32)
    w1_fwd[...] = jnp.concatenate([high, high, low], axis=0).T.astype(bf16)
    w2 = w2_ref[...]
    high, low = split(w2)
    w2_bwd[...] = jnp.concatenate([high, high, low], axis=1)
    high, low = split(w2.T)
    w2_fwd[...] = jnp.concatenate([high, high, low], axis=1)
    w3t = w3t_ref[...]
    high, low = split(w3t)
    w3_fwd[...] = jnp.concatenate([high, high, low], axis=1)
    high, low = high.astype(f32)[:8], low.astype(f32)[:8]
    w3_bwd[...] = jnp.concatenate([high, high, low, jnp.zeros_like(low)], axis=0).T.astype(bf16)
    acc_w1[...] = jnp.zeros_like(acc_w1)
    acc_w2[...] = jnp.zeros_like(acc_w2)
    acc_w3[...] = jnp.zeros_like(acc_w3)
    acc_b2[...] = jnp.zeros_like(acc_b2)
    acc_b3[...] = jnp.zeros_like(acc_b3)

    first.wait()
    merged = field_ref[half] + part_buf[...]
    fields = merged[:8]
    target = merged[8:]
    ocean = fields[6:7]
    state0 = jnp.where(sub < 5, fields * ocean, fields)

    def exchange(stage, to_east, to_west):
        edge_send[stage, 0] = to_east
        edge_send[stage, 1] = to_west
        copies = []
        for side, device in ((0, east), (1, west)):
            copy = pltpu.make_async_remote_copy(
                src_ref=edge_send.at[stage, side], dst_ref=edge_recv.at[stage, side],
                send_sem=edge_ssem.at[stage, side], recv_sem=edge_rsem.at[stage, side],
                device_id=device, device_id_type=MESH,
            )
            copy.start()
            copies.append(copy)
        return copies

    def lat_down(value):
        return jnp.where(low_edge, 0.0, pltpu.roll(value, 1, 1))

    def lat_up(value):
        return jnp.where(high_edge, 0.0, pltpu.roll(value, lanes - 1, 1))

    def factors(level):
        keep = jnp.where(level == 0, 0.0, jnp.where(level == 1, 0.75, 1.0 / 3.0)).astype(f32)
        move = jnp.where(level == 0, 1.0, jnp.where(level == 1, 0.25, 2.0 / 3.0)).astype(f32)
        return keep, move

    ones_group = jnp.where(sub == 0, 1.0, 0.0).astype(f32)

    def forward(stage, carry):
        current, start = carry
        level = stage % 3
        start = jnp.where(level == 0, current, start)
        from_west = pltpu.roll(current, row, 1)
        from_east = pltpu.roll(current, lanes - row, 1)
        copies = exchange(stage, from_west[:, :128], from_east[:, lanes - 128 :])
        centre = [lat_down(current), current, lat_up(current)]
        for copy in copies:
            copy.wait()
        west_side = jnp.concatenate(
            [jnp.where(lower_half, edge_recv[stage, 0], from_west[:, :128]), from_west[:, 128:]], axis=1
        )
        east_side = jnp.concatenate(
            [
                from_east[:, : lanes - 128],
                jnp.where(lower_half, from_east[:, lanes - 128 :], edge_recv[stage, 1]),
            ],
            axis=1,
        )
        groups = (
            [lat_down(west_side), west_side, lat_up(west_side)]
            + centre
            + [lat_down(east_side), east_side, lat_up(east_side)]
        )
        feats = jnp.concatenate(groups + [ones_group], axis=0)
        tape_f[stage] = feats
        hidden_one = jnp.tanh(matmul(w1_fwd[...], stacked(feats)))
        tape_h1[stage] = hidden_one
        hidden_two = jnp.tanh(matmul(w2_fwd[...], stacked(hidden_one)) + b2_ref[...])
        tape_h2[stage] = hidden_two
        closure = matmul(w3_fwd[...], stacked(hidden_two))[:8] + b3_ref[...]
        we, ea, so, no = groups[1], groups[7], groups[3], groups[5]
        laplace = ea + we + no + so - 4.0 * current
        dx, dy = ea - we, no - so
        u, v = current[1:2], current[2:3]
        rate_h = -0.5 * (ea[5:6] * ea[1:2] - we[5:6] * we[1:2] + no[5:6] * no[2:3] - so[5:6] * so[2:3])
        rate_u = coriolis * v - 0.5 * dx[0:1] - 0.05 * u + 0.05 * laplace[1:2]
        rate_v = -coriolis * u - 0.5 * dy[0:1] - 0.05 * v + 0.05 * laplace[2:3]
        rate_t = 0.05 * laplace - 0.5 * (u * dx + v * dy)
        rates = jnp.where(sub == 0, rate_h, jnp.where(sub == 1, rate_u, jnp.where(sub == 2, rate_v, rate_t)))
        rates = (rates + closure) * ocean
        keep, move = factors(level)
        moved = keep * start + move * (current + time_step * rates)
        return jnp.where(sub < 5, moved, current), start

    final, _ = lax.fori_loop(0, LEVELS, forward, (state0, state0))
    error = jnp.where(sub < 5, final - target, 0.0)
    adjoint = ocean * error
    misfit = 0.5 * jnp.sum(jnp.sum(adjoint * error, axis=1, keepdims=True), axis=0, keepdims=True)

    def backward(index, carry):
        adjoint, start_total = carry
        stage = LEVELS - 1 - index
        slot = LEVELS + index
        level = stage % 3
        keep, move = factors(level)
        start_total = jnp.where(level == 2, 0.0, start_total) + keep * adjoint
        grad = (move * time_step) * adjoint * ocean
        feats = tape_f[stage]
        hidden_one = tape_h1[stage]
        hidden_two = tape_h2[stage]
        high, low = split(grad)
        high, low = high.astype(f32), low.astype(f32)
        grad_stack = jnp.concatenate([high, low, high, jnp.zeros_like(high)], axis=0).astype(bf16)
        dz2 = matmul(w3_bwd[...], grad_stack) * (1.0 - hidden_two * hidden_two)
        dz2_high, dz2_low = split(dz2)
        dz1 = matmul(w2_bwd[...], jnp.concatenate([dz2_high, dz2_low, dz2_high], axis=0)) * (
            1.0 - hidden_one * hidden_one
        )
        dz1_high, dz1_low = split(dz1)
        dfeats = matmul(w1_bwd[...], jnp.concatenate([dz1_high, dz1_low, dz1_high], axis=0))
        we, ea, so, no, ce = feats[8:16], feats[56:64], feats[24:32], feats[40:48], feats[32:40]
        dx, dy = ea - we, no - so
        u, v = ce[1:2], ce[2:3]
        gh, gu, gv = grad[0:1], grad[1:2], grad[2:3]
        gt = jnp.where(sub >= 3, grad, 0.0)
        lap = jnp.where(sub >= 1, 0.05 * grad, 0.0)
        ugt, vgt = u * gt, v * gt
        d_ea = lap - 0.5 * jnp.where(sub == 0, gu, jnp.where(sub == 1, gh * ea[5:6], ugt))
        d_we = lap + 0.5 * jnp.where(sub == 0, gu, jnp.where(sub == 1, gh * we[5:6], ugt))
        d_no = lap - 0.5 * jnp.where(sub == 0, gv, jnp.where(sub == 2, gh * no[5:6], vgt))
        d_so = lap + 0.5 * jnp.where(sub == 0, gv, jnp.where(sub == 2, gh * so[5:6], vgt))
        du = -coriolis * gv - 0.05 * gu - 0.5 * jnp.sum(gt * dx, axis=0, keepdims=True)
        dv = coriolis * gu - 0.05 * gv - 0.5 * jnp.sum(gt * dy, axis=0, keepdims=True)
        d_ce = jnp.where(sub == 1, du, jnp.where(sub == 2, dv, 0.0)) - 4.0 * lap
        part = [dfeats[8 * i : 8 * i + 8] for i in range(9)]
        to_west = lat_up(part[0]) + (part[1] + d_we) + lat_down(part[2])
        to_east = lat_up(part[6]) + (part[7] + d_ea) + lat_down(part[8])
        stay = lat_up(part[3] + d_so) + (part[4] + d_ce) + lat_down(part[5] + d_no)
        to_west = pltpu.roll(to_west, lanes - row, 1)
        to_east = pltpu.roll(to_east, row, 1)
        copies = exchange(
            slot,
            jnp.where(lower_half, to_east[:, :128], 0.0),
            jnp.where(lower_half, 0.0, to_west[:, lanes - 128 :]),
        )
        result = (
            move * adjoint
            + stay
            + jnp.where(lane < row, 0.0, to_east)
            + jnp.where(lane >= lanes - row, 0.0, to_west)
        )
        h1_high, h1_low = split(hidden_one)
        acc_w2[...] += matmul_t(
            jnp.concatenate([h1_high, h1_high, h1_low], axis=1),
            jnp.concatenate([dz2_high, dz2_low, dz2_high], axis=1),
        )
        f_high, f_low = split(feats)
        acc_w1[...] += matmul_t(
            jnp.concatenate([f_high, f_high, f_low], axis=1),
            jnp.concatenate([dz1_high, dz1_low, dz1_high], axis=1),
        )
        h2_high, h2_low = split(hidden_two)
        g16 = jnp.concatenate([grad, jnp.zeros_like(grad)], axis=0)
        g_high, g_low = split(g16)
        acc_w3[...] += matmul_t(
            jnp.concatenate([g_high, g_high, g_low], axis=1),
            jnp.concatenate([h2_high, h2_low, h2_high], axis=1),
        )[:8]
        acc_b2[...] += sum(dz2[:, i : i + 128] for i in range(0, lanes, 128))
        acc_b3[...] += sum(grad[:, i : i + 128] for i in range(0, lanes, 128))
        for copy in copies:
            copy.wait()
        result = jnp.concatenate(
            [result[:, :128] + edge_recv[slot, 0]]
            + [result[:, i : i + 128] for i in range(128, lanes - 128, 128)]
            + [result[:, lanes - 128 :] + edge_recv[slot, 1]],
            axis=1,
        )
        result = jnp.where(level == 0, result + start_total, result)
        return result, start_total

    adjoint, _ = lax.fori_loop(0, LEVELS, backward, (adjoint, jnp.zeros_like(adjoint)))
    adj_out[half] = adjoint * ocean

    f_row = lax.broadcasted_iota(jnp.int32, (FROWS, HID), 0)
    real = ((f_row < 72) & (f_row % 8 < 5)) | (f_row == 72)
    sub_w = lax.broadcasted_iota(jnp.int32, (8, HID), 0)
    lane_w = lax.broadcasted_iota(jnp.int32, (8, HID), 1)
    b2_row = jnp.sum(acc_b2[...].T, axis=0, keepdims=True)
    b3_col = jnp.sum(acc_b3[...], axis=1, keepdims=True)
    tile_b2 = jnp.where(sub_w == 0, b2_row, 0.0)
    tile_b3 = jnp.where(lane_w == 0, jnp.where(sub_w == 5, misfit, jnp.where(sub_w < 5, b3_col, 0.0)), 0.0)
    extra = peers * chunk - (HID + FROWS + 24)
    pieces = [acc_w2[...], jnp.where(real, acc_w1[...], 0.0), acc_w3[...], tile_b2, tile_b3]
    if extra:
        pieces.append(jnp.zeros((extra, HID), f32))
    grad_buf[...] = jnp.concatenate(pieces, axis=0).reshape(peers, chunk, HID)

    back = pltpu.make_async_remote_copy(
        src_ref=adj_out.at[half], dst_ref=adj_out.at[half],
        send_sem=back_sem.at[0], recv_sem=back_sem.at[1],
        device_id=partner, device_id_type=MESH,
    )

    def scatter(step):
        to = (me + step) % peers
        return pltpu.make_async_remote_copy(
            src_ref=grad_buf.at[to], dst_ref=reduce_buf.at[step],
            send_sem=rs_ssem.at[step], recv_sem=rs_rsem.at[step],
            device_id=place(to), device_id_type=MESH,
        )

    def gather(step):
        to = (me + step) % peers
        return pltpu.make_async_remote_copy(
            src_ref=gather_buf.at[me], dst_ref=gather_buf.at[me],
            send_sem=ag_ssem.at[step], recv_sem=ag_rsem.at[step],
            device_id=place(to), device_id_type=MESH,
        )

    def loop(body, init):
        return lax.fori_loop(1, peers, body, init, unroll=peers <= 16)

    def start_of(make):
        def body(step, carry):
            make(step).start()
            return carry

        return body

    loop(start_of(scatter), 0)
    back.start()

    def take(step, total):
        scatter(step).wait_recv()
        return total + reduce_buf[step]

    gather_buf[me] = loop(take, grad_buf[me])
    loop(start_of(gather), 0)

    def arrive(step, carry):
        source = (me + peers - step) % peers
        pltpu.make_async_remote_copy(
            src_ref=gather_buf.at[source], dst_ref=gather_buf.at[source],
            send_sem=ag_ssem.at[step], recv_sem=ag_rsem.at[step],
            device_id=place((me + step) % peers), device_id_type=MESH,
        ).wait_recv()
        return carry

    loop(arrive, 0)
    summed = gather_buf[...].reshape(peers * chunk, HID)
    base = HID + FROWS + 16
    is_loss = (sub_w == 5) & (lane_w == 0)
    last = summed[base : base + 8]
    square = summed[:base] * summed[:base]
    total = jnp.sum(jnp.sum(square, axis=0, keepdims=True), axis=1, keepdims=True)
    rest = jnp.where(is_loss, 0.0, last * last)
    total = total + jnp.sum(jnp.sum(rest, axis=0, keepdims=True), axis=1, keepdims=True)
    scale = 1.0 / jnp.sqrt(total / number + eps_norm)
    w2_out[...] = summed[:HID] * scale
    for i in range(9):
        w1_out[5 * i : 5 * i + 5] = summed[HID + 8 * i : HID + 8 * i + 5] * scale
    b1_out[...] = summed[HID + 72 : HID + 73] * scale
    w3_out[...] = (summed[HID + FROWS : HID + FROWS + 8] * scale).T[:, :5]
    b2_out[...] = summed[HID + FROWS + 8 : HID + FROWS + 9] * scale
    b3_out[...] = (last * scale)[:, :1]
    loss_out[...] = last[5:6, :1] / cells_total

    back.wait()

    def drain(step, carry):
        scatter(step).wait_send()
        gather(step).wait_send()
        return carry

    loop(drain, 0)


def on_device(state, target, depth, land_mask, w_one, b_one, w_two, b_two, w_three, b_three):
    half = lax.axis_index("lat")
    halves = lax.axis_size("lat")
    peers = lax.axis_size("lon") * halves
    cells_lon, cells_lat = depth.shape
    row = cells_lat * halves
    lines = cells_lon // halves
    lanes = lines * row
    ocean = (1 - land_mask).astype(f32)
    zero = jnp.zeros((1, cells_lon, cells_lat), f32)
    block = jnp.concatenate(
        [state, depth[None], ocean[None], zero, target, jnp.zeros((3, cells_lon, cells_lat), f32)], axis=0
    )
    block = jnp.concatenate(
        [jnp.where(half == 0, block, 0.0), jnp.where(half == 1, block, 0.0)], axis=2
    )
    fields = block.reshape(16, halves, lanes).transpose(1, 0, 2)
    w1 = jnp.pad(w_one.reshape(9, 5, HID), ((0, 0), (0, 3), (0, 0))).reshape(72, HID)
    w1 = jnp.concatenate([w1, b_one[None], jnp.zeros((FROWS - 73, HID), f32)], axis=0)
    w3t = jnp.pad(w_three.T, ((0, 11), (0, 0)))
    b2 = b_two[:, None]
    b3 = jnp.pad(b_three, (0, 3))[:, None]
    number = w_one.size + b_one.size + w_two.size + b_two.size + w_three.size + b_three.size
    used = HID + FROWS + 24
    chunk = -(-used // peers)
    chunk = -(-chunk // 8) * 8
    shape = jax.ShapeDtypeStruct
    vmem = pl.BlockSpec(memory_space=pltpu.VMEM)
    dma = pltpu.SemaphoreType.DMA
    cells_total = peers // halves * cells_lon * row
    outs = pl.pallas_call(
        functools.partial(kernel, peers, chunk, row, float(number), float(cells_total)),
        out_shape=(
            shape((1, 1), f32), shape((2, 8, lanes), f32), shape((45, HID), f32), shape((1, HID), f32),
            shape((HID, HID), f32), shape((1, HID), f32), shape((HID, 5), f32), shape((8, 1), f32),
        ),
        in_specs=[vmem] * 6,
        out_specs=(vmem,) * 8,
        scratch_shapes=[
            pltpu.VMEM((16, lanes), f32),
            pltpu.VMEM((2 * LEVELS, 2, 8, 128), f32),
            pltpu.VMEM((2 * LEVELS, 2, 8, 128), f32),
            pltpu.VMEM((LEVELS, FROWS, lanes), f32),
            pltpu.VMEM((LEVELS, HID, lanes), f32),
            pltpu.VMEM((LEVELS, HID, lanes), f32),
            pltpu.VMEM((HID, 3 * FROWS), bf16),
            pltpu.VMEM((FROWS, 3 * HID), bf16),
            pltpu.VMEM((HID, 3 * HID), bf16),
            pltpu.VMEM((HID, 3 * HID), bf16),
            pltpu.VMEM((16, 3 * HID), bf16),
            pltpu.VMEM((HID, 32), bf16),
            pltpu.VMEM((FROWS, HID), f32),
            pltpu.VMEM((HID, HID), f32),
            pltpu.VMEM((8, HID), f32),
            pltpu.VMEM((HID, 128), f32),
            pltpu.VMEM((8, 128), f32),
            pltpu.VMEM((peers, chunk, HID), f32),
            pltpu.VMEM((peers, chunk, HID), f32),
            pltpu.VMEM((peers, chunk, HID), f32),
            dma((2,)),
            dma((2 * LEVELS, 2)),
            dma((2 * LEVELS, 2)),
            dma((2,)),
            dma((peers,)),
            dma((peers,)),
            dma((peers,)),
            dma((peers,)),
        ],
        compiler_params=pltpu.CompilerParams(
            collective_id=0, has_side_effects=True, vmem_limit_bytes=40 * 1024 * 1024
        ),
    )(fields, w1, w_two, w3t, b2, b3)
    loss, adjoint, d1, e1, d2, e2, d3, e3 = outs
    adjoint = adjoint[:, :5].reshape(2, 5, lines, row).transpose(1, 0, 2, 3).reshape(5, cells_lon, row)
    adjoint = jnp.where(half == 0, adjoint[:, :, :cells_lat], adjoint[:, :, cells_lat:])
    return (
        loss.reshape(1), adjoint, d1, e1.reshape(HID), d2, e2.reshape(HID), d3, e3[:5, 0],
    )


def solution(mesh):
    in_specs = (
        P(None, ("grp", "lon"), "lat"),
        P(None, ("grp", "lon"), "lat"),
        P(("grp", "lon"), "lat"),
        P(("grp", "lon"), "lat"),
    ) + (P(),) * 6
    out_specs = (
        P("grp"),
        P(None, ("grp", "lon"), "lat"),
        P("grp", None),
        P("grp"),
        P("grp", None),
        P("grp"),
        P("grp", None),
        P("grp"),
    )
    return jax.shard_map(
        on_device, mesh=mesh, in_specs=in_specs, out_specs=out_specs, check_vma=False
    )
```

profile of v0, /device:TPU:0, one launch (start us, length us, event | category | flops | bytes accessed | tf_op | source)
XLA Modules:
  0.0 88.1 jit_solution(10890995660375107361)
XLA Ops:
  0.6 0.7 pad_bitcast_fusion.1
  1.3 0.1 pad.17.clone
  1.4 0.1 copy.23.b3_ref
  1.5 0.7 pad.13.w3t_ref
  2.2 0.0 copy-start.6
  2.2 0.7 copy-done.6
  2.9 0.1 maximum_maximum_fusion.w1_ref
  3.0 0.7 copy-done.2
  3.7 0.7 copy-done.4
  4.4 0.7 copy-done.5
  5.1 0.1 pad_maximum_fusion
  5.2 0.0 copy-start
  5.2 0.1 reshape.40
  5.4 0.7 copy-done.7
  6.0 0.1 copy.22.b2_ref
  6.2 75.6 %shard_map.161 = (f32[1,1]{1,0:T(1,128)}, f32[2,8,384]{2,1,0:T(8,128)S(1)}, f32[45,256]{1,0:T(8,128)S(1)}, f32[1,256]{1,0:T(1,128)S(1)}, f32[256,256]{1,0:T(8,12...) custom-call(f32[2,16,384]{2,1,0:T(8,128)S(1)} %bitcast.21, ...), custom_call_target="tpu_custom_call" | custom-call | tf_op jit(solution)/shard_map/pallas_call | solution.py:403
  81.8 0.6 slice_reduce_fusion
  82.4 0.7 copy.25
  83.1 0.1 reshape.44
  83.2 0.7 slice_select_fusion
  84.5 0.6 copy.39
  85.1 0.6 copy.40
  85.7 0.7 copy.41
  86.4 0.6 copy.42
  (22 shorter events, 0.1 us)
Async XLA Ops:
  0.6 1.5 %copy-start.1 = (f32[45,256]{1,0:T(8,128)S(1)}, f32[45,256]{1,0:T(8,128)}, u32[]{:S(2)}) copy-start(f32[45,256]{1,0:T(8,128)} %param.14) | copy-start | bytes 138244
  2.2 0.7 copy-start.6
  2.9 0.8 copy-start.2
  3.7 0.7 copy-start.4
  3.7 1.4 %copy-start.3 = (f32[5,12,32]{2,1,0:T(8,128)S(1)}, f32[5,12,32]{2,1,0:T(8,128)}, u32[]{:S(2)}) copy-start(f32[5,12,32]{2,1,0:T(8,128)} %param.11) | copy-start | bytes 23044
  4.3 0.7 copy-start.5
  5.2 1.0 %copy-start = (f32[256,256]{1,0:T(8,128)S(1)}, f32[256,256]{1,0:T(8,128)}, u32[]{:S(2)}) copy-start(f32[256,256]{1,0:T(8,128)} %w2_ref.1) | copy-start | bytes 786436
  5.3 0.7 copy-start.7
where the time goes:
time: 89.5 us; the launch traced here: 88.1 us
  Pallas kernels  75.6 us (84%)
  local copies, waits for them, and re-layouts  9.08 us (10%)
  between operations  2.46 us (3%)
  other arithmetic  0.9 us (1%)
    pallas_call x1, Pallas kernels, on_device(): pl.pallas_call(functools.partial(kernel, peers, chunk, row, float(number)...  75.6 us
    unnamed x25, local copies, waits for them, and re-layouts  6.57 us

commit v1 on v0

--- a/solution.py
+++ b/solution.py
@@ -39,25 +39,30 @@
 
 def kernel(
     peers, chunk, row, number, cells_total,
-    field_ref, w1_ref, w2_ref, w3t_ref, b2_ref, b3_ref,
+    field_ref, w1_ref, b1_ref, w2_ref, b2_ref, w3_ref, b3_ref,
     loss_out, adj_out, w1_out, b1_out, w2_out, b2_out, w3_out, b3_out,
-    part_buf, edge_send, edge_recv, tape_f, tape_h1, tape_h2,
+    w1_pad, w3_pad, b2_col, adj_src, part_buf, edge_send, edge_recv, tape_f, tape_h1, tape_h2,
     w1_fwd, w1_bwd, w2_fwd, w2_bwd, w3_fwd, w3_bwd,
     acc_w1, acc_w2, acc_w3, acc_b2, acc_b3,
     grad_buf, reduce_buf, gather_buf,
-    part_sem, edge_ssem, edge_rsem, back_sem, rs_ssem, rs_rsem, ag_ssem, ag_rsem,
+    part_ssem, part_rsem, edge_ssem, edge_rsem, back_ssem, back_rsem, rs_ssem, rs_rsem, ag_ssem, ag_rsem,
 ):
     grp = lax.axis_index("grp")
     lon = lax.axis_index("lon")
     half = lax.axis_index("lat")
-    me = lon * 2 + half
+    snake = peers == 16
+
+    def chip_at(spot):
+        return jnp.where(spot < 4, 2 * spot, 15 - 2 * spot) if snake else spot
+
+    spot = jnp.where(lon % 2 == 0, lon // 2, 7 - lon // 2) if snake else lon
+    me = spot * 2 + half
 
     def place(position):
-        return (grp, position // 2, position % 2)
+        return (grp, chip_at(position // 2), position % 2)
 
     east = place((me + 1) % peers)
     west = place((me + peers - 1) % peers)
-    partner = (grp, lon, 1 - half)
 
     barrier = pltpu.get_barrier_semaphore()
 
@@ -68,12 +73,36 @@
     lax.fori_loop(1, peers, greet, 0, unroll=peers <= 16)
     pl.semaphore_wait(barrier, peers - 1)
 
-    first = pltpu.make_async_remote_copy(
-        src_ref=field_ref.at[1 - half], dst_ref=part_buf,
-        send_sem=part_sem.at[0], recv_sem=part_sem.at[1],
-        device_id=partner, device_id_type=MESH,
-    )
-    first.start()
+    def spread(side):
+        return pltpu.make_async_remote_copy(
+            src_ref=field_ref.at[side], dst_ref=part_buf.at[half],
+            send_sem=part_ssem.at[side], recv_sem=part_rsem.at[half],
+            device_id=(grp, chip_at(lon), side), device_id_type=MESH,
+        )
+
+    def arrival(side):
+        return pltpu.make_async_remote_copy(
+            src_ref=field_ref.at[side], dst_ref=part_buf.at[side],
+            send_sem=part_ssem.at[side], recv_sem=part_rsem.at[side],
+            device_id=(grp, chip_at(lon), side), device_id_type=MESH,
+        )
+
+    at_home = spot == lon
+
+    def remote(side):
+        return jnp.logical_not(at_home & (half == side))
+
+    def own(side):
+        return at_home & (half == side)
+
+    for side in range(2):
+        @pl.when(remote(side))
+        def _(side=side):
+            spread(side).start()
+
+        @pl.when(own(side))
+        def _(side=side):
+            part_buf[side] = field_ref[side]
 
     lanes = field_ref.shape[2]
     lane = lax.broadcasted_iota(jnp.int32, (8, lanes), 1)
@@ -85,7 +114,16 @@
     lower_half = lane_tile < row
     coriolis = (0.2 + 0.6 * (latitude.astype(f32) + 0.5) / row)[0:1]
 
-    w1 = w1_ref[...]
+    w1_pad[...] = jnp.zeros_like(w1_pad)
+    for i in range(9):
+        w1_pad[8 * i : 8 * i + 5] = w1_ref[5 * i : 5 * i + 5]
+    w1_pad[72:73] = b1_ref[...]
+    w3_pad[...] = jnp.zeros_like(w3_pad)
+    w3_pad[:, :5] = w3_ref[...]
+    b2_col[...] = jnp.broadcast_to(b2_ref[...], (128, HID)).T
+    corner = lax.broadcasted_iota(jnp.int32, (8, 5), 0) == lax.broadcasted_iota(jnp.int32, (8, 5), 1)
+    bias_three = jnp.sum(jnp.where(corner, b3_ref[...], 0.0), axis=1, keepdims=True)
+    w1 = w1_pad[...]
     high, low = split(w1)
     w1_bwd[...] = jnp.concatenate([high, high, low], axis=1)
     high, low = high.astype(f32), low.astype(f32)
@@ -95,7 +133,7 @@
     w2_bwd[...] = jnp.concatenate([high, high, low], axis=1)
     high, low = split(w2.T)
     w2_fwd[...] = jnp.concatenate([high, high, low], axis=1)
-    w3t = w3t_ref[...]
+    w3t = w3_pad[...].T[:16]
     high, low = split(w3t)
     w3_fwd[...] = jnp.concatenate([high, high, low], axis=1)
     high, low = high.astype(f32)[:8], low.astype(f32)[:8]
@@ -106,8 +144,12 @@
     acc_b2[...] = jnp.zeros_like(acc_b2)
     acc_b3[...] = jnp.zeros_like(acc_b3)
 
-    first.wait()
-    merged = field_ref[half] + part_buf[...]
+    for side in range(2):
+        @pl.when(remote(side))
+        def _(side=side):
+            arrival(side).wait()
+
+    merged = part_buf[0] + part_buf[1]
     fields = merged[:8]
     target = merged[8:]
     ocean = fields[6:7]
@@ -169,9 +211,9 @@
         tape_f[stage] = feats
         hidden_one = jnp.tanh(matmul(w1_fwd[...], stacked(feats)))
         tape_h1[stage] = hidden_one
-        hidden_two = jnp.tanh(matmul(w2_fwd[...], stacked(hidden_one)) + b2_ref[...])
+        hidden_two = jnp.tanh(matmul(w2_fwd[...], stacked(hidden_one)) + b2_col[:, :1])
         tape_h2[stage] = hidden_two
-        closure = matmul(w3_fwd[...], stacked(hidden_two))[:8] + b3_ref[...]
+        closure = matmul(w3_fwd[...], stacked(hidden_two))[:8] + bias_three
         we, ea, so, no = groups[1], groups[7], groups[3], groups[5]
         laplace = ea + we + no + so - 4.0 * current
         dx, dy = ea - we, no - so
@@ -274,7 +316,7 @@
         return result, start_total
 
     adjoint, _ = lax.fori_loop(0, LEVELS, backward, (adjoint, jnp.zeros_like(adjoint)))
-    adj_out[half] = adjoint * ocean
+    adj_src[...] = adjoint * ocean
 
     f_row = lax.broadcasted_iota(jnp.int32, (FROWS, HID), 0)
     real = ((f_row < 72) & (f_row % 8 < 5)) | (f_row == 72)
@@ -290,11 +332,12 @@
         pieces.append(jnp.zeros((extra, HID), f32))
     grad_buf[...] = jnp.concatenate(pieces, axis=0).reshape(peers, chunk, HID)
 
-    back = pltpu.make_async_remote_copy(
-        src_ref=adj_out.at[half], dst_ref=adj_out.at[half],
-        send_sem=back_sem.at[0], recv_sem=back_sem.at[1],
-        device_id=partner, device_id_type=MESH,
-    )
+    def back(side, slot):
+        return pltpu.make_async_remote_copy(
+            src_ref=adj_src, dst_ref=adj_out.at[slot],
+            send_sem=back_ssem.at[side], recv_sem=back_rsem.at[slot],
+            device_id=(grp, spot, side), device_id_type=MESH,
+        )
 
     def scatter(step):
         to = (me + step) % peers
@@ -323,7 +366,14 @@
         return body
 
     loop(start_of(scatter), 0)
-    back.start()
+    for side in range(2):
+        @pl.when(remote(side))
+        def _(side=side):
+            back(side, half).start()
+
+        @pl.when(own(side))
+        def _(side=side):
+            adj_out[side] = adj_src[...]
 
     def take(step, total):
         scatter(step).wait_recv()
@@ -360,7 +410,10 @@
     b3_out[...] = (last * scale)[:, :1]
     loss_out[...] = last[5:6, :1] / cells_total
 
-    back.wait()
+    for side in range(2):
+        @pl.when(remote(side))
+        def _(side=side):
+            back(side, side).wait()
 
     def drain(step, carry):
         scatter(step).wait_send()
@@ -387,11 +440,6 @@
         [jnp.where(half == 0, block, 0.0), jnp.where(half == 1, block, 0.0)], axis=2
     )
     fields = block.reshape(16, halves, lanes).transpose(1, 0, 2)
-    w1 = jnp.pad(w_one.reshape(9, 5, HID), ((0, 0), (0, 3), (0, 0))).reshape(72, HID)
-    w1 = jnp.concatenate([w1, b_one[None], jnp.zeros((FROWS - 73, HID), f32)], axis=0)
-    w3t = jnp.pad(w_three.T, ((0, 11), (0, 0)))
-    b2 = b_two[:, None]
-    b3 = jnp.pad(b_three, (0, 3))[:, None]
     number = w_one.size + b_one.size + w_two.size + b_two.size + w_three.size + b_three.size
     used = HID + FROWS + 24
     chunk = -(-used // peers)
@@ -406,10 +454,14 @@
             shape((1, 1), f32), shape((2, 8, lanes), f32), shape((45, HID), f32), shape((1, HID), f32),
             shape((HID, HID), f32), shape((1, HID), f32), shape((HID, 5), f32), shape((8, 1), f32),
         ),
-        in_specs=[vmem] * 6,
+        in_specs=[vmem] * 7,
         out_specs=(vmem,) * 8,
         scratch_shapes=[
-            pltpu.VMEM((16, lanes), f32),
+            pltpu.VMEM((FROWS, HID), f32),
+            pltpu.VMEM((HID, 128), f32),
+            pltpu.VMEM((HID, 128), f32),
+            pltpu.VMEM((8, lanes), f32),
+            pltpu.VMEM((2, 16, lanes), f32),
             pltpu.VMEM((2 * LEVELS, 2, 8, 128), f32),
             pltpu.VMEM((2 * LEVELS, 2, 8, 128), f32),
             pltpu.VMEM((LEVELS, FROWS, lanes), f32),
@@ -430,8 +482,10 @@
             pltpu.VMEM((peers, chunk, HID), f32),
             pltpu.VMEM((peers, chunk, HID), f32),
             dma((2,)),
+            dma((2,)),
             dma((2 * LEVELS, 2)),
             dma((2 * LEVELS, 2)),
+            dma((2,)),
             dma((2,)),
             dma((peers,)),
             dma((peers,)),
@@ -441,7 +495,7 @@
         compiler_params=pltpu.CompilerParams(
             collective_id=0, has_side_effects=True, vmem_limit_bytes=40 * 1024 * 1024
         ),
-    )(fields, w1, w_two, w3t, b2, b3)
+    )(fields, w_one, b_one[None], w_two, b_two[None], w_three, b_three[None])
     loss, adjoint, d1, e1, d2, e2, d3, e3 = outs
     adjoint = adjoint[:, :5].reshape(2, 5, lines, row).transpose(1, 0, 2, 3).reshape(5, cells_lon, row)
     adjoint = jnp.where(half == 0, adjoint[:, :, :cells_lat], adjoint[:, :, cells_lat:])

time: 89.5 us -> 79.8 us (0.89); the launches traced: 88.1 us -> 79.5 us
  Pallas kernels: 75.6 us -> 69.2 us
  local copies, waits for them, and re-layouts: 9.08 us -> 6.96 us
    pallas_call x1, Pallas kernels: 75.6 us -> 69.2 us  [on_device(): pl.pallas_call(functools.partial(kernel, peers, chunk, row, float(number)...]
    unnamed x25 -> x28, local copies, waits for them, and re-layouts: 6.57 us -> 6.12 us
where the time goes in v1:
time: 79.8 us; the launch traced here: 79.5 us
  Pallas kernels  69.2 us (87%)
  local copies, waits for them, and re-layouts  6.96 us (9%)
  between operations  2.57 us (3%)
  other arithmetic  0.82 us (1%)
    pallas_call x1, Pallas kernels, on_device(): pl.pallas_call(functools.partial(kernel, peers, chunk, row, float(number)...  69.2 us
    unnamed x28, local copies, waits for them, and re-layouts  6.12 us

profile of v1, /device:TPU:0, one launch (start us, length us, event | category | flops | bytes accessed | tf_op | source)
XLA Modules:
  0.0 79.5 jit_solution(11081232383816577206)
XLA Ops:
  0.6 0.0 copy-start.7
  0.6 0.0 copy-start.5
  0.7 0.8 %constant_dynamic-update-slice_fusion.5 = f32[16,12,32]{2,1,0:T(8,128)S(1)} fusion(f32[5,12,32]{2,1,0:T(8,128)} %param.10), kind=kLoop, calls=%fused_computation.10 | loop fusion | bytes 48640
  1.5 0.0 copy-done.7
  1.5 0.7 copy-done.8
  2.2 0.0 copy-done.5
  2.2 0.1 pad_maximum_fusion
  2.3 0.0 copy-start
  2.3 0.1 reshape.34
  2.4 0.0 copy-start.6
  2.5 0.7 copy-done.6
  3.1 0.1 copy.22.w3_ref
  3.3 0.0 copy-done
  3.3 0.7 copy-done.1
  4.0 0.0 copy-done.3
  4.0 69.2 %shard_map.161 = (f32[1,1]{1,0:T(1,128)}, f32[2,8,384]{2,1,0:T(8,128)S(1)}, f32[45,256]{1,0:T(8,128)S(1)}, f32[1,256]{1,0:T(1,128)S(1)}, f32[256,256]{1,0:T(8,12...) custom-call(f32[2,16,384]{2,1,0:T(8,128)S(1)} %bitcast.17, f32[45,256]{1,0:T(8,128)S(1)} %copy-done.1, ...), custom_call_target="tpu_custom_call" | custom-call | tf_op jit(solution)/shard_map/pallas_call | solution.py:451
  73.1 0.6 slice_reduce_fusion
  73.8 0.7 copy.24
  74.5 0.1 reshape.36
  74.5 0.7 slice_select_fusion
  75.9 0.6 copy.38
  76.6 0.6 copy.39
  77.1 0.7 copy.40
  77.8 0.6 copy.41
  (16 shorter events, 0.1 us)
Async XLA Ops:
  0.6 0.8 %copy-start.7 = (f32[12,32]{1,0:T(8,128)S(1)}, f32[12,32]{1,0:T(8,128)}, u32[]{:S(2)}) copy-start(f32[12,32]{1,0:T(8,128)} %param.12) | copy-start | bytes 4612
  0.6 1.5 %copy-start.5 = (f32[5,12,32]{2,1,0:T(8,128)S(1)}, f32[5,12,32]{2,1,0:T(8,128)}, u32[]{:S(2)}) copy-start(f32[5,12,32]{2,1,0:T(8,128)} %param.11) | copy-start | bytes 23044
  1.5 0.7 copy-start.8
  2.3 1.0 %copy-start = (f32[256,256]{1,0:T(8,128)S(1)}, f32[256,256]{1,0:T(8,128)}, u32[]{:S(2)}) copy-start(f32[256,256]{1,0:T(8,128)} %w2_ref.1) | copy-start | bytes 786436
  2.4 0.7 copy-start.6
  3.1 0.8 %copy-start.1 = (f32[45,256]{1,0:T(8,128)S(1)}, f32[45,256]{1,0:T(8,128)}, u32[]{:S(2)}) copy-start(f32[45,256]{1,0:T(8,128)} %w1_ref.1) | copy-start | bytes 138244
  3.1 0.8 %copy-start.2 = (f32[256]{0:T(256)S(1)}, f32[256]{0:T(256)}, u32[]{:S(2)}) copy-start(f32[256]{0:T(256)} %param.15) | copy-start | bytes 3076
  3.1 0.8 %copy-start.3 = (f32[256]{0:T(256)S(1)}, f32[256]{0:T(256)}, u32[]{:S(2)}) copy-start(f32[256]{0:T(256)} %param.17) | copy-start | bytes 3076
  3.1 0.8 %copy-start.4 = (f32[5]{0:T(128)S(1)}, f32[5]{0:T(128)}, u32[]{:S(2)}) copy-start(f32[5]{0:T(128)} %param.19) | copy-start | bytes 64

commit v2 on v1

--- a/solution.py
+++ b/solution.py
@@ -180,55 +180,65 @@
         move = jnp.where(level == 0, 1.0, jnp.where(level == 1, 0.25, 2.0 / 3.0)).astype(f32)
         return keep, move
 
-    ones_group = jnp.where(sub == 0, 1.0, 0.0).astype(f32)
-
-    def forward(stage, carry):
-        current, start = carry
-        level = stage % 3
-        start = jnp.where(level == 0, current, start)
-        from_west = pltpu.roll(current, row, 1)
-        from_east = pltpu.roll(current, lanes - row, 1)
-        copies = exchange(stage, from_west[:, :128], from_east[:, lanes - 128 :])
-        centre = [lat_down(current), current, lat_up(current)]
-        for copy in copies:
-            copy.wait()
-        west_side = jnp.concatenate(
-            [jnp.where(lower_half, edge_recv[stage, 0], from_west[:, :128]), from_west[:, 128:]], axis=1
-        )
-        east_side = jnp.concatenate(
-            [
-                from_east[:, : lanes - 128],
-                jnp.where(lower_half, from_east[:, lanes - 128 :], edge_recv[stage, 1]),
-            ],
-            axis=1,
-        )
-        groups = (
-            [lat_down(west_side), west_side, lat_up(west_side)]
-            + centre
-            + [lat_down(east_side), east_side, lat_up(east_side)]
-        )
-        feats = jnp.concatenate(groups + [ones_group], axis=0)
-        tape_f[stage] = feats
+    outer = lanes + 256
+
+    def evolve(stage, level, around, start, wide):
+        width = outer if wide else lanes
+        first_lane = 0 if wide else 128
+
+        def cut(value):
+            return value[:, first_lane : first_lane + width]
+
+        rows = lax.broadcasted_iota(jnp.int32, (8, width), 0)
+        lats = lax.broadcasted_iota(jnp.int32, (8, width), 1) % row
+
+        def south_of(value):
+            return jnp.where(lats == 0, 0.0, pltpu.roll(value, 1, 1))
+
+        def north_of(value):
+            return jnp.where(lats == row - 1, 0.0, pltpu.roll(value, width - 1, 1))
+
+        current = cut(around)
+        start = cut(start)
+        groups = []
+        for side in (cut(pltpu.roll(around, row, 1)), current, cut(pltpu.roll(around, outer - row, 1))):
+            groups += [south_of(side), side, north_of(side)]
+        feats = jnp.concatenate(groups + [jnp.where(rows == 0, 1.0, 0.0).astype(f32)], axis=0)
         hidden_one = jnp.tanh(matmul(w1_fwd[...], stacked(feats)))
-        tape_h1[stage] = hidden_one
         hidden_two = jnp.tanh(matmul(w2_fwd[...], stacked(hidden_one)) + b2_col[:, :1])
-        tape_h2[stage] = hidden_two
+        low_lane = 128 if wide else 0
+        tape_f[stage] = feats[:, low_lane : low_lane + lanes]
+        tape_h1[stage] = hidden_one[:, low_lane : low_lane + lanes]
+        tape_h2[stage] = hidden_two[:, low_lane : low_lane + lanes]
         closure = matmul(w3_fwd[...], stacked(hidden_two))[:8] + bias_three
         we, ea, so, no = groups[1], groups[7], groups[3], groups[5]
         laplace = ea + we + no + so - 4.0 * current
         dx, dy = ea - we, no - so
         u, v = current[1:2], current[2:3]
+        turn = (0.2 + 0.6 * (lats.astype(f32) + 0.5) / row)[0:1]
         rate_h = -0.5 * (ea[5:6] * ea[1:2] - we[5:6] * we[1:2] + no[5:6] * no[2:3] - so[5:6] * so[2:3])
-        rate_u = coriolis * v - 0.5 * dx[0:1] - 0.05 * u + 0.05 * laplace[1:2]
-        rate_v = -coriolis * u - 0.5 * dy[0:1] - 0.05 * v + 0.05 * laplace[2:3]
+        rate_u = turn * v - 0.5 * dx[0:1] - 0.05 * u + 0.05 * laplace[1:2]
+        rate_v = -turn * u - 0.5 * dy[0:1] - 0.05 * v + 0.05 * laplace[2:3]
         rate_t = 0.05 * laplace - 0.5 * (u * dx + v * dy)
-        rates = jnp.where(sub == 0, rate_h, jnp.where(sub == 1, rate_u, jnp.where(sub == 2, rate_v, rate_t)))
-        rates = (rates + closure) * ocean
+        rates = jnp.where(rows == 0, rate_h, jnp.where(rows == 1, rate_u, jnp.where(rows == 2, rate_v, rate_t)))
+        rates = (rates + closure) * current[6:7]
         keep, move = factors(level)
         moved = keep * start + move * (current + time_step * rates)
-        return jnp.where(sub < 5, moved, current), start
-
-    final, _ = lax.fori_loop(0, LEVELS, forward, (state0, state0))
+        return jnp.where(rows < 5, moved, current)
+
+    def forward(pair, carry):
+        current, start = carry
+        stage = 2 * pair
+        level, later = stage % 3, (stage + 1) % 3
+        for copy in exchange(stage, current[:, lanes - 128 :], current[:, :128]):
+            copy.wait()
+        around = jnp.concatenate([edge_recv[stage, 0], current, edge_recv[stage, 1]], axis=1)
+        start = jnp.where(level == 0, around, start)
+        around = evolve(stage, level, around, start, True)
+        start = jnp.where(later == 0, around, start)
+        return evolve(stage + 1, later, around, start, False), start
+
+    final, _ = lax.fori_loop(0, LEVELS // 2, forward, (state0, jnp.zeros((8, outer), f32)))
     error = jnp.where(sub < 5, final - target, 0.0)
     adjoint = ocean * error
     misfit = 0.5 * jnp.sum(jnp.sum(adjoint * error, axis=1, keepdims=True), axis=0, keepdims=True)

time: 79.8 us -> 73.2 us (0.917)
  Pallas kernels: 69.2 us -> 62.5 us
    pallas_call x1, Pallas kernels: 69.2 us -> 62.5 us  [on_device(): pl.pallas_call(functools.partial(kernel, peers, chunk, row, float(number)...]
where the time goes in v2:
time: 73.2 us; the launch traced here: 72.9 us
  Pallas kernels  62.5 us (85%)
  local copies, waits for them, and re-layouts  6.96 us (10%)
  between operations  2.57 us (4%)
  other arithmetic  0.82 us (1%)
    pallas_call x1, Pallas kernels, on_device(): pl.pallas_call(functools.partial(kernel, peers, chunk, row, float(number)...  62.5 us
    unnamed x28, local copies, waits for them, and re-layouts  6.12 us

profile of v2, /device:TPU:0, one launch (start us, length us, event | category | flops | bytes accessed | tf_op | source)
XLA Modules:
  0.0 72.9 jit_solution(8359978500808858542)
XLA Ops:
  0.6 0.0 copy-start.7
  0.6 0.0 copy-start.5
  0.7 0.8 %constant_dynamic-update-slice_fusion.5 = f32[16,12,32]{2,1,0:T(8,128)S(1)} fusion(f32[5,12,32]{2,1,0:T(8,128)} %param.10), kind=kLoop, calls=%fused_computation.10 | loop fusion | bytes 48640
  1.5 0.0 copy-done.7
  1.5 0.7 copy-done.8
  2.2 0.0 copy-done.5
  2.2 0.1 pad_maximum_fusion
  2.3 0.0 copy-start
  2.3 0.1 reshape.34
  2.4 0.0 copy-start.6
  2.5 0.7 copy-done.6
  3.1 0.1 copy.22.w3_ref
  3.3 0.0 copy-done
  3.3 0.7 copy-done.1
  4.0 0.0 copy-done.2
  4.0 62.5 %shard_map.161 = (f32[1,1]{1,0:T(1,128)}, f32[2,8,384]{2,1,0:T(8,128)S(1)}, f32[45,256]{1,0:T(8,128)S(1)}, f32[1,256]{1,0:T(1,128)S(1)}, f32[256,256]{1,0:T(8,12...) custom-call(f32[2,16,384]{2,1,0:T(8,128)S(1)} %bitcast.17, f32[45,256]{1,0:T(8,128)S(1)} %copy-done.1, ...), custom_call_target="tpu_custom_call" | custom-call | tf_op jit(solution)/shard_map/pallas_call | solution.py:461
  66.5 0.6 slice_reduce_fusion
  67.1 0.7 copy.24
  67.8 0.1 reshape.36
  67.9 0.7 slice_select_fusion
  69.3 0.6 copy.38
  69.9 0.6 copy.39
  70.5 0.7 copy.40
  71.2 0.6 copy.41
  (16 shorter events, 0.1 us)
Async XLA Ops:
  0.6 0.8 %copy-start.7 = (f32[12,32]{1,0:T(8,128)S(1)}, f32[12,32]{1,0:T(8,128)}, u32[]{:S(2)}) copy-start(f32[12,32]{1,0:T(8,128)} %param.12) | copy-start | bytes 4612
  0.6 1.5 %copy-start.5 = (f32[5,12,32]{2,1,0:T(8,128)S(1)}, f32[5,12,32]{2,1,0:T(8,128)}, u32[]{:S(2)}) copy-start(f32[5,12,32]{2,1,0:T(8,128)} %param.11) | copy-start | bytes 23044
  1.5 0.7 copy-start.8
  2.3 1.0 %copy-start = (f32[256,256]{1,0:T(8,128)S(1)}, f32[256,256]{1,0:T(8,128)}, u32[]{:S(2)}) copy-start(f32[256,256]{1,0:T(8,128)} %w2_ref.1) | copy-start | bytes 786436
  2.4 0.7 copy-start.6
  3.1 0.8 %copy-start.1 = (f32[45,256]{1,0:T(8,128)S(1)}, f32[45,256]{1,0:T(8,128)}, u32[]{:S(2)}) copy-start(f32[45,256]{1,0:T(8,128)} %w1_ref.1) | copy-start | bytes 138244
  3.1 0.8 %copy-start.2 = (f32[256]{0:T(256)S(1)}, f32[256]{0:T(256)}, u32[]{:S(2)}) copy-start(f32[256]{0:T(256)} %param.15) | copy-start | bytes 3076
  3.1 0.8 %copy-start.3 = (f32[256]{0:T(256)S(1)}, f32[256]{0:T(256)}, u32[]{:S(2)}) copy-start(f32[256]{0:T(256)} %param.17) | copy-start | bytes 3076
  3.1 0.8 %copy-start.4 = (f32[5]{0:T(128)S(1)}, f32[5]{0:T(128)}, u32[]{:S(2)}) copy-start(f32[5]{0:T(128)} %param.19) | copy-start | bytes 64

commit v3 on v2

--- a/solution.py
+++ b/solution.py
@@ -40,8 +40,8 @@
 def kernel(
     peers, chunk, row, number, cells_total,
     field_ref, w1_ref, b1_ref, w2_ref, b2_ref, w3_ref, b3_ref,
-    loss_out, adj_out, w1_out, b1_out, w2_out, b2_out, w3_out, b3_out,
-    w1_pad, w3_pad, b2_col, adj_src, part_buf, edge_send, edge_recv, tape_f, tape_h1, tape_h2,
+    loss_out, block_out, w1_out, b1_out, w2_out, b2_out, w3_out, b3_out,
+    w1_pad, w3_pad, b2_col, adj_out, adj_src, part_buf, edge_send, edge_recv, tape_f, tape_h1, tape_h2,
     w1_fwd, w1_bwd, w2_fwd, w2_bwd, w3_fwd, w3_bwd,
     acc_w1, acc_w2, acc_w3, acc_b2, acc_b3,
     grad_buf, reduce_buf, gather_buf,
@@ -425,6 +425,14 @@
         def _(side=side):
             back(side, side).wait()
 
+    lines = lanes // row
+    for side in range(2):
+        whole = adj_out[side][:5]
+        for line in range(lines):
+            left = whole[:, line * row : line * row + row // 2]
+            right = whole[:, line * row + row // 2 : (line + 1) * row]
+            block_out[:, side * lines + line, :] = jnp.where(half == 0, left, right)
+
     def drain(step, carry):
         scatter(step).wait_send()
         gather(step).wait_send()
@@ -461,7 +469,7 @@
     outs = pl.pallas_call(
         functools.partial(kernel, peers, chunk, row, float(number), float(cells_total)),
         out_shape=(
-            shape((1, 1), f32), shape((2, 8, lanes), f32), shape((45, HID), f32), shape((1, HID), f32),
+            shape((1, 1), f32), shape((5, cells_lon, cells_lat), f32), shape((45, HID), f32), shape((1, HID), f32),
             shape((HID, HID), f32), shape((1, HID), f32), shape((HID, 5), f32), shape((8, 1), f32),
         ),
         in_specs=[vmem] * 7,
@@ -470,6 +478,7 @@
             pltpu.VMEM((FROWS, HID), f32),
             pltpu.VMEM((HID, 128), f32),
             pltpu.VMEM((HID, 128), f32),
+            pltpu.VMEM((2, 8, lanes), f32),
             pltpu.VMEM((8, lanes), f32),
             pltpu.VMEM((2, 16, lanes), f32),
             pltpu.VMEM((2 * LEVELS, 2, 8, 128), f32),
@@ -507,8 +516,6 @@
         ),
     )(fields, w_one, b_one[None], w_two, b_two[None], w_three, b_three[None])
     loss, adjoint, d1, e1, d2, e2, d3, e3 = outs
-    adjoint = adjoint[:, :5].reshape(2, 5, lines, row).transpose(1, 0, 2, 3).reshape(5, cells_lon, row)
-    adjoint = jnp.where(half == 0, adjoint[:, :, :cells_lat], adjoint[:, :, cells_lat:])
     return (
         loss.reshape(1), adjoint, d1, e1.reshape(HID), d2, e2.reshape(HID), d3, e3[:5, 0],
     )

time: 73.2 us -> 73.2 us (level)
    unnamed x28 -> x29, local copies, waits for them, and re-layouts: 6.12 us -> 6.74 us
where the time goes in v3:
time: 73.2 us; the launch traced here: 72.9 us
  Pallas kernels  62.8 us (86%)
  local copies, waits for them, and re-layouts  7.47 us (10%)
  between operations  2.57 us (4%)
    pallas_call x1, Pallas kernels, on_device(): pl.pallas_call(functools.partial(kernel, peers, chunk, row, float(number)...  62.8 us
    unnamed x29, local copies, waits for them, and re-layouts  6.74 us

profile of v3, /device:TPU:0, one launch (start us, length us, event | category | flops | bytes accessed | tf_op | source)
XLA Modules:
  0.0 72.9 jit_solution(18272291511886540896)
XLA Ops:
  0.6 0.0 copy-start.7
  0.6 0.0 copy-start.5
  0.7 0.8 %constant_dynamic-update-slice_fusion.5 = f32[16,12,32]{2,1,0:T(8,128)S(1)} fusion(f32[5,12,32]{2,1,0:T(8,128)} %param.10), kind=kLoop, calls=%fused_computation.9 | loop fusion | bytes 48640
  1.5 0.0 copy-done.7
  1.5 0.7 copy-done.8
  2.2 0.0 copy-done.5
  2.2 0.1 pad_maximum_fusion
  2.3 0.0 copy-start
  2.3 0.1 reshape.28
  2.4 0.0 copy-start.6
  2.5 0.7 copy-done.6
  3.1 0.1 copy.21.w3_ref
  3.3 0.0 copy-done
  3.3 0.7 copy-done.1
  4.0 0.0 copy-done.2
  4.0 0.0 copy-done.3
  4.0 62.8 %shard_map.161 = (f32[1,1]{1,0:T(1,128)}, f32[5,12,32]{2,1,0:T(8,128)S(1)}, f32[45,256]{1,0:T(8,128)S(1)}, f32[1,256]{1,0:T(1,128)S(1)}, f32[256,256]{1,0:T(8,12...) custom-call(f32[2,16,384]{2,1,0:T(8,128)S(1)} %bitcast.13, f32[45,256]{1,0:T(8,128)S(1)} %copy-done.1, ...), custom_call_target="tpu_custom_call" | custom-call | tf_op jit(solution)/shard_map/pallas_call | solution.py:469
  66.7 0.6 slice_reduce_fusion
  67.4 0.7 copy.22
  68.7 0.6 copy.37
  69.3 0.6 copy.38
  70.0 0.6 copy.39
  70.5 0.7 copy.40
  71.2 0.6 copy.41
  (13 shorter events, 0.1 us)
Async XLA Ops:
  0.6 0.8 %copy-start.7 = (f32[12,32]{1,0:T(8,128)S(1)}, f32[12,32]{1,0:T(8,128)}, u32[]{:S(2)}) copy-start(f32[12,32]{1,0:T(8,128)} %param.12) | copy-start | bytes 4612
  0.6 1.5 %copy-start.5 = (f32[5,12,32]{2,1,0:T(8,128)S(1)}, f32[5,12,32]{2,1,0:T(8,128)}, u32[]{:S(2)}) copy-start(f32[5,12,32]{2,1,0:T(8,128)} %param.11) | copy-start | bytes 23044
  1.5 0.7 copy-start.8
  2.3 1.0 %copy-start = (f32[256,256]{1,0:T(8,128)S(1)}, f32[256,256]{1,0:T(8,128)}, u32[]{:S(2)}) copy-start(f32[256,256]{1,0:T(8,128)} %w2_ref.1) | copy-start | bytes 786436
  2.4 0.7 copy-start.6
  3.1 0.8 %copy-start.1 = (f32[45,256]{1,0:T(8,128)S(1)}, f32[45,256]{1,0:T(8,128)}, u32[]{:S(2)}) copy-start(f32[45,256]{1,0:T(8,128)} %w1_ref.1) | copy-start | bytes 138244
  3.1 0.8 %copy-start.2 = (f32[256]{0:T(256)S(1)}, f32[256]{0:T(256)}, u32[]{:S(2)}) copy-start(f32[256]{0:T(256)} %param.15) | copy-start | bytes 3076
  3.1 0.8 %copy-start.3 = (f32[256]{0:T(256)S(1)}, f32[256]{0:T(256)}, u32[]{:S(2)}) copy-start(f32[256]{0:T(256)} %param.17) | copy-start | bytes 3076
  3.1 0.8 %copy-start.4 = (f32[5]{0:T(128)S(1)}, f32[5]{0:T(128)}, u32[]{:S(2)}) copy-start(f32[5]{0:T(128)} %param.19) | copy-start | bytes 64
